TPU v7x, 32 devices: a whole 2x2x4 slice. The times are simulated.
32 devices in a mesh: expert: 16 (over z, y, x), dp: 2 (over core).
Axes of the slice: x: 2, y: 2, z: 4, core: 2. Of those that a mesh axis runs over, the one named last changes fastest.
Arguments:
- tokens: bfloat16 [2048, 3584], P('expert'), may hold values from -6 to 6
- expert_ids: int32 [2048, 8], P('expert'), may hold values from 0 to 15, all different within a row; in each aligned block of 128 rows (0 to 127, 128 to 255, ...) at most 96 rows name the same one
- route_weights: float32 [2048, 8], P('expert'), may hold values from 0.05 to 0.45
- gate_up_panels: bfloat16 [16, 2, 1792, 2048], P('expert', 'dp'), may hold values from -0.09375 to 0.09375
- down_panels: bfloat16 [16, 1024, 3584], P('expert', None, 'dp'), may hold values from -0.1875 to 0.1875
- partner: int32 [16], replicated, may hold values from 0 to 15, as said below
Outputs:
- moe_out: bfloat16 [2048, 3584], P('expert', 'dp')
- new_gate_up: bfloat16 [16, 2, 1792, 2048], P('expert', 'dp')
- new_down: bfloat16 [16, 1024, 3584], P('expert', None, 'dp')
Inputs may be any that keep to these rules, and one draw needn't show every extreme that they name: `expert_ids`: in the 128 rows of one index of the expert axis, each row names 8 different experts and no expert is named by more than 96 rows. partner[i] is i, i XOR 1 or i XOR 2, the same of these for the four indices of each aligned group of four; partner[partner[i]] = i; some group takes XOR 1 and some group XOR 2.
All inputs are finite; a program needn't handle non-finite values.
Results may differ from a plain program's by a relative error of at most 0.0057.
Values may be sent and summed in bfloat16 or wider, within the bound.
A program may use at most 128 MiB of HBM per device.

v0:
```python
import jax
import jax.numpy as jnp
from jax import lax
from jax.sharding import PartitionSpec as P


def from_partner(block, axis, bit):
    count = lax.axis_size(axis)
    route = []
    for low in range(count):
        high = low | 1 << bit
        if high != low and high < count:
            route += [(low, high), (high, low)]
    return lax.ppermute(block, axis, route)


def swap_panels(gate_up, down, partner):
    here = lax.axis_index("expert")
    partner_id = partner[here]
    result_gate_up, result_down = (gate_up, down)
    for bit_number in range(2):
        moved_gate_up, moved_down = from_partner((gate_up, down), "expert", bit_number)
        taken = partner_id == jnp.bitwise_xor(here, 1 << bit_number)
        result_gate_up = jnp.where(taken, moved_gate_up, result_gate_up)
        result_down = jnp.where(taken, moved_down, result_down)
    return (result_gate_up, result_down)


def run_layer(tokens, expert_ids, route_weights, gate_up, down, owner_table):
    devices = lax.axis_size("expert")
    token_rows, model_width = tokens.shape
    top_count = expert_ids.shape[1]
    expert_count = owner_table.shape[0]
    capacity = min(token_rows, 3 * token_rows * top_count // (2 * expert_count))
    half_width = model_width // 2
    side = lax.rem(lax.axis_index("dp"), 2)
    own_half = lax.dynamic_slice_in_dim(tokens, side * half_width, half_width, 1)
    labels = jnp.arange(expert_count, dtype=jnp.int32)
    onehot = (expert_ids[:, :, None] == labels[None, None, :]).astype(jnp.int32)
    picked = jnp.sum(onehot, axis=1)
    slot_rank = jnp.cumsum(picked, axis=0) - picked
    slots = jnp.sum(onehot * slot_rank[:, None, :], axis=2)
    target = jnp.sum(onehot * owner_table[None, None, :], axis=2)
    place = (target * capacity + slots).reshape(-1)
    row_ids = jnp.repeat(jnp.arange(token_rows, dtype=jnp.int32), top_count)
    source = jnp.full((devices * capacity,), token_rows, jnp.int32).at[place].set(row_ids)
    padded = jnp.concatenate([own_half, jnp.zeros((1, half_width), own_half.dtype)], axis=0)
    outgoing = padded[source].reshape(devices, capacity, half_width)
    arrived = lax.all_to_all(outgoing, "expert", split_axis=0, concat_axis=0, tiled=True)
    flat = arrived.reshape(devices * capacity, half_width)
    partial_value = jnp.dot(flat, gate_up, preferred_element_type=jnp.float32)
    half_rows = flat.shape[0] // 2
    mine = lax.dynamic_slice_in_dim(partial_value, side * half_rows, half_rows, 0)
    other = lax.dynamic_slice_in_dim(partial_value, (1 - side) * half_rows, half_rows, 0)
    summed = mine + from_partner(other, "dp", 0)
    block_units = gate_up.shape[1] // 2
    hidden = (jax.nn.silu(summed[:, :block_units]) * summed[:, block_units:]).astype(jnp.bfloat16)
    gathered = lax.all_gather(hidden, "dp", axis=1, tiled=True)
    pair_count = lax.axis_size("dp") // 2
    out_columns = down.shape[1]
    outputs = jnp.einsum(
        "rqhk,qkc->hrc",
        gathered.reshape(half_rows, pair_count, 2, block_units),
        down.reshape(pair_count, block_units, out_columns),
        preferred_element_type=jnp.float32,
    )
    expert_out = outputs.reshape(devices, capacity, out_columns).astype(jnp.bfloat16)
    returned = lax.all_to_all(expert_out, "expert", split_axis=0, concat_axis=0, tiled=True)
    chosen = returned.reshape(devices * capacity, out_columns)[place].reshape(
        token_rows, top_count, out_columns
    )
    mixed = jnp.sum(chosen.astype(jnp.float32) * route_weights[:, :, None], axis=1)
    return mixed.astype(jnp.bfloat16)


def per_device(tokens, expert_ids, route_weights, gate_up_panels, down_panels, partner):
    new_gate_up, new_down = swap_panels(gate_up_panels, down_panels, partner)
    moe_out = run_layer(tokens, expert_ids, route_weights, new_gate_up[0, 0], new_down[0], partner)
    return (moe_out, new_gate_up, new_down)


def solution(mesh):
    return jax.shard_map(
        per_device,
        mesh=mesh,
        in_specs=(
            P("expert", None),
            P("expert", None),
            P("expert", None),
            P("expert", "dp", None, None),
            P("expert", None, "dp"),
            P(),
        ),
        out_specs=(P("expert", "dp"), P("expert", "dp", None, None), P("expert", None, "dp")),
        check_vma=False,
    )
```

profile of v0, /device:TPU:14, one launch (start us, length us, event | category | flops | bytes accessed | tf_op | source)
XLA Modules:
  0.0 533.2 jit_solution(12265515958487995451)
XLA Ops:
  7.2 0.8 convert_reduce_fusion
  8.0 0.1 copy.15
  8.1 0.2 reduce_window_sum.11
  8.3 0.8 select_reduce_fusion.1
  9.1 0.1 copy.18
  9.2 0.1 add.55
  9.4 0.1 reshape.105
  9.5 4.3 scatter_custom_fusion
  13.9 6.8 %gather_fusion = bf16[1536,1792]{1,0:T(8,128)(2,1)} fusion(bf16[129,1792]{1,0:T(8,128)(2,1)S(1)} %concatenate.3, s32[2048]{0:T(1024)S(1)} %pad_clamp_fusion), kind=kCustom, calls=%fused_computation | custom fusion | bytes 11016192 | tf_op jit(solution)/shard_map/gather | solution.py:48
  20.7 7.3 %all-to-all-start = ((bf16[16,96,1792]{2,1,0:T(8,128)(2,1)}), bf16[16,96,1792]{2,1,0:T(8,128)(2,1)}, u32[]{:S(2)}, u32[]{:S(2)}) async-start(bf16[16,96,1792]{2,1,0:T(8,128)(2,1)} %bitcast.23), calls=%async_computation | async-start | bytes 11010048 | tf_op jit(solution)/shard_map/all_to_all | solution.py:49
  28.0 0.2 all-gather.2.cloned.1.call-start
  28.2 0.6 collective-permute-start.2
  28.8 0.6 collective-permute-start.3
  29.4 0.6 dynamic_slice.12
  31.3 214.0 %collective-permute-done.2 = bf16[1,1,1792,2048]{3,2,1,0:T(8,128)(2,1)} collective-permute-done((bf16[1,1,1792,2048]{3,2,1,0:T(8,128)(2,1)}, bf16[1,1,1792,2048]{3,2,1,0:T(8,128)(2,1)}, u32[]{:S(2)}, u32[]{:S(2)}) %collective-permute-start.2) | collective-permute-done | bytes 7340064 | tf_op jit(solution)/shard_map/ppermute | solution.py:14
  245.3 3.8 collective-permute-done.3
  249.1 6.7 %select_select_fusion = bf16[1,1,1792,2048]{3,2,1,0:T(8,128)(2,1)} fusion(bf16[1,1,1792,2048]{3,2,1,0:T(8,128)(2,1)} %collective-permute-done.2, bf16[1,1,1792,2048]{3,2,1,0:T(8,128)(2,1)} %collective-permute-done.3, bf16[1,1,1792,2048]{3,2,1,0:T(8,128)(2,1)} %param.9, pred[]{:T(512)S(6)} %eq.20, pred[]{:T(512)S(6)} %eq.19), kind=kLoop, calls=%fused_computation.7 | loop fusion | flops 7340032 | bytes 29360130 | tf_op jit(solution)/shard_map/jit(_where)/select_n | solution.py:24
  255.8 16.1 %fusion.1 = f32[1536,2048]{1,0:T(8,128)S(1)} fusion(bf16[1536,1792]{1,0:T(8,128)(2,1)} %bitcast.5, bf16[1,1,1792,2048]{3,2,1,0:T(8,128)(2,1)} %select_select_fusion), kind=kOutput, calls=%fused_computation.5 | convolution fusion | flops 11274289152 | bytes 25427968 | tf_op jit(solution)/shard_map/dot_general | solution.py:51
  271.9 3.3 constant_dynamic-slice_fusion
  275.2 3.2 copy-done.2
  278.5 0.3 collective-permute-start
  278.7 10.2 %collective-permute-done.4 = f32[768,2048]{1,0:T(8,128)} collective-permute-done((f32[768,2048]{1,0:T(8,128)}, f32[768,2048]{1,0:T(8,128)}, u32[]{:S(2)}, u32[]{:S(2)}) %collective-permute-start.4) | collective-permute-done | bytes 6291488 | tf_op jit(solution)/shard_map/ppermute | solution.py:14
  288.9 5.9 %dynamic-slice_add_fusion = f32[768,2048]{1,0:T(8,128)S(1)} fusion(f32[768,2048]{1,0:T(8,128)} %collective-permute-done.4, f32[1536,2048]{1,0:T(8,128)} %copy-done.2, s32[]{:T(128)S(6)} %select_n.66), kind=kLoop, calls=%fused_computation.8 | loop fusion | flops 1572864 | bytes 18874372 | tf_op jit(solution)/shard_map/add | solution.py:55
  294.9 2.2 fusion.6
  297.0 63.5 %collective-permute-done = bf16[1,1024,1792]{2,1,0:T(8,128)(2,1)} collective-permute-done((bf16[1,1024,1792]{2,1,0:T(8,128)(2,1)}, bf16[1,1024,1792]{2,1,0:T(8,128)(2,1)}, u32[]{:S(2)}, u32[]{:S(2)}) %collective-permute-start) | collective-permute-done | bytes 3670048 | tf_op jit(solution)/shard_map/ppermute | solution.py:14
  360.5 4.4 select_select_fusion.1
  364.9 10.1 %convolution_convert_fusion = bf16[1792,768,2]{0,1,2:T(8,128)(2,1)} fusion(bf16[1,1024,1792]{2,1,0:T(8,128)(2,1)} %select_select_fusion.1, bf16[96,2,8,1024]{3,2,1,0:T(8,128)(2,1)} %bitcast.27), kind=kOutput, calls=%fused_computation.9 | convolution fusion | flops 5639897088 | bytes 12320768 | tf_op jit(solution)/shard_map/rqhk,qkc->hrc/dot_general | solution.py:61
  375.0 10.7 %all-to-all-start.1 = ((bf16[16,96,1792]{2,1,0:T(8,128)(2,1)}), bf16[16,96,1792]{2,1,0:T(8,128)(2,1)}, u32[]{:S(2)}, u32[]{:S(2)}) async-start(bf16[16,96,1792]{2,1,0:T(8,128)(2,1)} %bitcast.24), calls=%async_computation.1 | async-start | bytes 11010048 | tf_op jit(solution)/shard_map/all_to_all | solution.py:68
  385.7 0.1 copy.20
  385.8 123.1 %all-to-all-done.1 = bf16[16,96,1792]{2,1,0:T(8,128)(2,1)} async-done(((bf16[16,96,1792]{2,1,0:T(8,128)(2,1)}), bf16[16,96,1792]{2,1,0:T(8,128)(2,1)}, u32[]{:S(2)}, u32[]{:S(2)}) %all-to-all-start.1) | async-done | bytes 5505056 | tf_op jit(solution)/shard_map/all_to_all | solution.py:68
  508.9 11.3 %gather_fusion.1 = bf16[1024,1792]{1,0:T(8,128)(2,1)} fusion(bf16[1536,1792]{1,0:T(8,128)(2,1)} %bitcast.9, s32[1024]{0:T(1024)S(1)} %broadcast_clamp_fusion), kind=kCustom, calls=%fused_computation.1 | custom fusion | bytes 7344128 | tf_op jit(solution)/shard_map/gather | solution.py:69
  520.3 6.1 %fusion = bf16[128,1792]{1,0:T(8,128)(2,1)} fusion(bf16[1024,1792]{1,0:T(8,128)(2,1)} %gather_fusion.1, f32[128,8]{1,0:T(8,128)S(1)} %copy.20), kind=kLoop, calls=%fused_computation.4 | loop fusion | flops 5275648 | bytes 4132864 | tf_op jit(solution)/shard_map/reduce_sum | solution.py:72
  (25 shorter events, 0.2 us)
Async XLA Ops:
  7.2 6.7 %copy-start = (bf16[128,3584]{1,0:T(8,128)(2,1)S(1)}, bf16[128,3584]{1,0:T(8,128)(2,1)}, u32[]{:S(2)}) copy-start(bf16[128,3584]{1,0:T(8,128)(2,1)} %param.6) | copy-start | bytes 2752516
  20.7 8.7 %copy-start.4 = (s32[16]{0:T(128)S(1)}, s32[16]{0:T(128)}, u32[]{:S(2)}) copy-start(s32[16]{0:T(128)} %param.11) | copy-start | bytes 196
  20.7 235.1 %all-to-all-start = ((bf16[16,96,1792]{2,1,0:T(8,128)(2,1)}), bf16[16,96,1792]{2,1,0:T(8,128)(2,1)}, u32[]{:S(2)}, u32[]{:S(2)}) async-start(bf16[16,96,1792]{2,1,0:T(8,128)(2,1)} %bitcast.23), calls=%async_computation | async-start | bytes 11010048 | tf_op jit(solution)/shard_map/all_to_all | solution.py:49
  28.0 336.9 %all-gather.2.cloned.1.call-start = ((), (), s32[]{:S(2)}) async-start(), calls=%async_computation.2 | async-start | bytes 4718592 | tf_op jit(solution)/shard_map/all_gather | solution.py:58
  28.2 217.1 %collective-permute-start.2 = (bf16[1,1,1792,2048]{3,2,1,0:T(8,128)(2,1)}, bf16[1,1,1792,2048]{3,2,1,0:T(8,128)(2,1)}, u32[]{:S(2)}, u32[]{:S(2)}) collective-permute-start(bf16[1,1,1792,2048]{3,2,1,0:T(8,128)(2,1)} %param.9), channel_id=1, source_target_pairs={{0,4},{4,0},{2,6},{6,2},{8,12},{12,8},{10,14},{14,10},{16,20},{20,... | collective-permute-start | bytes 22020104 | tf_op jit(solution)/shard_map/ppermute | solution.py:14
  28.8 220.2 %collective-permute-start.3 = (bf16[1,1,1792,2048]{3,2,1,0:T(8,128)(2,1)}, bf16[1,1,1792,2048]{3,2,1,0:T(8,128)(2,1)}, u32[]{:S(2)}, u32[]{:S(2)}) collective-permute-start(bf16[1,1,1792,2048]{3,2,1,0:T(8,128)(2,1)} %param.9), channel_id=1, source_target_pairs={{0,2},{2,0},{4,6},{6,4},{8,10},{10,8},{12,14},{14,12},{16,18},{18,... | collective-permute-start | bytes 22020104 | tf_op jit(solution)/shard_map/ppermute | solution.py:14
  271.9 6.5 %copy-start.2 = (f32[1536,2048]{1,0:T(8,128)}, f32[1536,2048]{1,0:T(8,128)S(1)}, u32[]{:S(2)}) copy-start(f32[1536,2048]{1,0:T(8,128)S(1)} %fusion.1) | copy-start | bytes 37748740
  278.4 10.5 %collective-permute-start.4 = (f32[768,2048]{1,0:T(8,128)}, f32[768,2048]{1,0:T(8,128)}, u32[]{:S(2)}, u32[]{:S(2)}) collective-permute-start(f32[768,2048]{1,0:T(8,128)} %constant_dynamic-slice_fusion), channel_id=1, source_target_pairs={{0,1},{1,0},{2,3},{3,2},{4,5},{5,4},{6,7},{7,6},{8,9},{9,8},{10,11... | collective-permute-start | bytes 18874376 | tf_op jit(solution)/shard_map/ppermute | solution.py:14
  278.5 82.1 %collective-permute-start = (bf16[1,1024,1792]{2,1,0:T(8,128)(2,1)}, bf16[1,1024,1792]{2,1,0:T(8,128)(2,1)}, u32[]{:S(2)}, u32[]{:S(2)}) collective-permute-start(bf16[1,1024,1792]{2,1,0:T(8,128)(2,1)} %param.10), channel_id=1, source_target_pairs={{0,4},{4,0},{2,6},{6,2},{8,12},{12,8},{10,14},{14,10},{16,20},{20,... | collective-permute-start | bytes 11010056 | tf_op jit(solution)/shard_map/ppermute | solution.py:14
  278.7 81.8 %collective-permute-start.1 = (bf16[1,1024,1792]{2,1,0:T(8,128)(2,1)}, bf16[1,1024,1792]{2,1,0:T(8,128)(2,1)}, u32[]{:S(2)}, u32[]{:S(2)}) collective-permute-start(bf16[1,1024,1792]{2,1,0:T(8,128)(2,1)} %param.10), channel_id=1, source_target_pairs={{0,2},{2,0},{4,6},{6,4},{8,10},{10,8},{12,14},{14,12},{16,18},{18,... | collective-permute-start | bytes 11010056 | tf_op jit(solution)/shard_map/ppermute | solution.py:14
  375.0 10.7 %copy-start.3 = (f32[128,8]{0,1:T(8,128)S(1)}, f32[128,8]{0,1:T(8,128)}, u32[]{:S(2)}) copy-start(f32[128,8]{0,1:T(8,128)} %param.8) | copy-start | bytes 12292
  375.0 133.9 %all-to-all-start.1 = ((bf16[16,96,1792]{2,1,0:T(8,128)(2,1)}), bf16[16,96,1792]{2,1,0:T(8,128)(2,1)}, u32[]{:S(2)}, u32[]{:S(2)}) async-start(bf16[16,96,1792]{2,1,0:T(8,128)(2,1)} %bitcast.24), calls=%async_computation.1 | async-start | bytes 11010048 | tf_op jit(solution)/shard_map/all_to_all | solution.py:68
  508.9 17.4 %copy-start.1 = (bf16[128,3584]{1,0:T(8,128)(2,1)S(1)}, bf16[128,3584]{1,0:T(8,128)(2,1)}, u32[]{:S(2)}) copy-start(bf16[128,3584]{1,0:T(8,128)(2,1)} %param.6) | copy-start | bytes 2752516
Sparse Core Ops, SparseCore 0:
  297.2 15.5 all-gather.1
where the time goes:
time: 534 us; the launch traced here: 533 us
  waiting for transfers between devices  415 us (78%)
  local copies, waits for them, and re-layouts  30.2 us (6%)
  other arithmetic  27.1 us (5%)
  matrix products  26.3 us (5%)
  starting transfers between devices  19.7 us (4%)
  between operations  15.5 us (3%)
    ppermute x5, waiting for transfers between devices, from_partner(): return lax.ppermute(block, axis, route)  291 us
    all_to_all x1, waiting for transfers between devices, run_layer(): lax.all_to_all(expert_out, 'expert', split_axis=0, concat_axis=0, tiled=T...  123 us
    dot_general x1, matrix products, run_layer(): partial_value = jnp.dot(flat, gate_up, preferred_element_type=jnp.float32)  16.1 us
    gather x1, local copies, waits for them, and re-layouts, run_layer(): returned.reshape(devices * capacity, out_columns)[place]  11.3 us
    all_to_all x1, starting transfers between devices, run_layer(): lax.all_to_all(expert_out, 'expert', split_axis=0, concat_axis=0, tiled=T...  10.7 us
  transfers between devices with their start and end apart: 8, of which 5 were waited for; matrix products, arithmetic and copies ran while one was open for 4% of the time, Pallas kernels for 0%

commit v1 on v0

v1 whole, which is shorter than its diff:
```python
import jax
import jax.numpy as jnp
from jax import lax
from jax.sharding import PartitionSpec as P


def from_partner(block, axis, bit):
    count = lax.axis_size(axis)
    route = []
    for low in range(count):
        high = low | 1 << bit
        if high != low and high < count:
            route += [(low, high), (high, low)]
    return lax.ppermute(block, axis, route)


def pick(own, moved, partner):
    here = lax.axis_index("expert")
    result = own
    for bit_number in range(2):
        taken = partner[here] == jnp.bitwise_xor(here, 1 << bit_number)
        result = jnp.where(taken, moved[bit_number], result)
    return result


def move(block):
    return [from_partner(block, "expert", bit_number) for bit_number in range(2)]


def joined(block):
    if lax.axis_size("dp") > 2:
        return lax.all_gather(block, "dp", axis=1, tiled=True)
    width = block.shape[1]
    side = lax.axis_index("dp")
    other = from_partner(block, "dp", 0)
    first = jnp.where(side == 0, block, other)
    second = jnp.where(side == 0, other, block)
    return jnp.concatenate([first, second], axis=1)


def expert_mlp(flat, gate_up, down, side, moved):
    partial_value = jnp.dot(flat, gate_up, preferred_element_type=jnp.float32)
    half_rows = flat.shape[0] // 2
    mine = lax.dynamic_slice_in_dim(partial_value, side * half_rows, half_rows, 0)
    other = lax.dynamic_slice_in_dim(partial_value, (1 - side) * half_rows, half_rows, 0)
    summed = mine + from_partner(other, "dp", 0)
    block_units = gate_up.shape[1] // 2
    hidden = (jax.nn.silu(summed[:, :block_units]) * summed[:, block_units:]).astype(jnp.bfloat16)
    gathered = joined(hidden)
    gathered, moved = lax.optimization_barrier((gathered, moved))
    pair_count = lax.axis_size("dp") // 2
    out_columns = down.shape[1]
    outputs = jnp.einsum(
        "rqhk,qkc->hrc",
        gathered.reshape(half_rows, pair_count, 2, block_units),
        down.reshape(pair_count, block_units, out_columns),
        preferred_element_type=jnp.float32,
    )
    return outputs.reshape(2 * half_rows, out_columns), moved


def run_layer(tokens, expert_ids, route_weights, gate_up, down, moved):
    devices = lax.axis_size("expert")
    token_rows, model_width = tokens.shape
    top_count = expert_ids.shape[1]
    capacity = min(token_rows, 3 * token_rows * top_count // (2 * devices))
    half_width = model_width // 2
    side = lax.rem(lax.axis_index("dp"), 2)
    own_half = lax.dynamic_slice_in_dim(tokens, side * half_width, half_width, 1)
    labels = jnp.arange(devices, dtype=jnp.int32)
    onehot = (expert_ids[:, :, None] == labels[None, None, :]).astype(jnp.int32)
    picked = jnp.sum(onehot, axis=1)
    earlier = jnp.tri(token_rows, k=-1, dtype=jnp.bfloat16)
    slot_rank = jnp.dot(earlier, picked.astype(jnp.bfloat16), preferred_element_type=jnp.float32).astype(jnp.int32)
    slots = jnp.sum(onehot * slot_rank[:, None, :], axis=2)
    place = (expert_ids * capacity + slots).reshape(-1)
    row_ids = jnp.repeat(jnp.arange(token_rows, dtype=jnp.int32), top_count)
    source = jnp.full((devices * capacity,), token_rows, jnp.int32).at[place].set(row_ids)
    padded = jnp.concatenate([own_half, jnp.zeros((1, half_width), own_half.dtype)], axis=0)
    outgoing = padded[source].reshape(devices, capacity, half_width)
    arrived = lax.all_to_all(outgoing, "expert", split_axis=0, concat_axis=0, tiled=True)
    flat = arrived.reshape(devices * capacity, half_width)
    (early, middle) = moved
    flat, early = lax.optimization_barrier((flat, early))
    outputs, middle = expert_mlp(flat, gate_up, down, side, middle)
    out_columns = down.shape[1]
    expert_out = outputs.reshape(devices, capacity, out_columns).astype(jnp.bfloat16)
    returned = lax.all_to_all(expert_out, "expert", split_axis=0, concat_axis=0, tiled=True)
    chosen = returned.reshape(devices * capacity, out_columns)[place].reshape(
        token_rows, top_count, out_columns
    )
    mixed = jnp.sum(chosen.astype(jnp.float32) * route_weights[:, :, None], axis=1)
    return mixed.astype(jnp.bfloat16), (early, middle)


def per_device(tokens, expert_ids, route_weights, gate_up_panels, down_panels, partner):
    cut = gate_up_panels.shape[2] // 7 * 4
    moe_out, moved = run_layer(
        tokens, expert_ids, route_weights, gate_up_panels[0, 0], down_panels[0], (move(gate_up_panels[:, :, :cut]), move(down_panels))
    )
    late = move(gate_up_panels[:, :, cut:])
    whole = [jnp.concatenate(parts, axis=2) for parts in zip(moved[0], late)]
    new_gate_up = pick(gate_up_panels, whole, partner)
    new_down = pick(down_panels, moved[1], partner)
    return (moe_out, new_gate_up, new_down)


def solution(mesh):
    return jax.shard_map(
        per_device,
        mesh=mesh,
        in_specs=(
            P("expert", None),
            P("expert", None),
            P("expert", None),
            P("expert", "dp", None, None),
            P("expert", None, "dp"),
            P(),
        ),
        out_specs=(P("expert", "dp"), P("expert", "dp", None, None), P("expert", None, "dp")),
        check_vma=False,
    )
```

time: 534 us -> 463 us (0.87)
  waiting for transfers between devices: 415 us -> 338 us
  between operations: 15.5 us -> 2.11 us
  other arithmetic: 27.1 us -> 38 us
  local copies, waits for them, and re-layouts: 30.2 us -> 39.1 us
    all_to_all x1, waiting for transfers between devices: 123 us -> 0.01 us  [run_layer(): lax.all_to_all(expert_out, 'expert', split_axis=0, concat_axis=0, tiled=T...]
    ppermute x5 -> x8, waiting for transfers between devices: 291 us -> 338 us  [from_partner(): return lax.ppermute(block, axis, route)]
    select_n x2 -> x3, other arithmetic: 11.1 us -> 20.8 us  [the longest x2 16.5 us: pick(): result = jnp.where(taken, moved[bit_number], result)]
    slice x0 -> x2, local copies, waits for them, and re-layouts: none -> 8.77 us  [the longest x1 4.79 us: per_device(): gate_up_panels[:, :, :cut]]
    dot_general x2 -> x3, matrix products: 26.3 us -> 25.9 us  [the longest x1 16.1 us: expert_mlp(): partial_value = jnp.dot(flat, gate_up, preferred_element_type=jnp.float32)]
  transfers between devices with their start and end apart: 8 -> 10, of which waited for: 5 -> 6; matrix products, arithmetic and copies ran while one was open for 4% -> 8% of each run, Pallas kernels for 0% -> 0%
where the time goes in v1:
time: 463 us; the launch traced here: 461 us
  waiting for transfers between devices  338 us (73%)
  local copies, waits for them, and re-layouts  39.1 us (8%)
  other arithmetic  38 us (8%)
  matrix products  25.9 us (6%)
  starting transfers between devices  17.8 us (4%)
    ppermute x8, waiting for transfers between devices, from_partner(): return lax.ppermute(block, axis, route)  338 us
    select_n x2, other arithmetic, pick(): result = jnp.where(taken, moved[bit_number], result)  16.5 us
    dot_general x1, matrix products, expert_mlp(): partial_value = jnp.dot(flat, gate_up, preferred_element_type=jnp.float32)  16.1 us
    gather x1, local copies, waits for them, and re-layouts, run_layer(): returned.reshape(devices * capacity, out_columns)[place]  11.4 us
    dot_general x1, matrix products, expert_mlp(): jnp.einsum('rqhk,qkc->hrc', gathered.reshape(half_rows, pair_count, 2, bl...  9.62 us
  transfers between devices with their start and end apart: 10, of which 6 were waited for; matrix products, arithmetic and copies ran while one was open for 8% of the time, Pallas kernels for 0%

profile of v1, /device:TPU:14, one launch (start us, length us, event | category | flops | bytes accessed | tf_op | source)
XLA Modules:
  0.0 461.4 jit_solution(14363264810733716661)
XLA Ops:
  0.7 0.8 convert_reduce_fusion
  1.7 0.7 select_reduce_fusion
  2.4 0.7 multiply_add_fusion
  3.4 4.3 scatter_custom_fusion
  7.9 6.6 %gather_fusion = bf16[1536,1792]{1,0:T(8,128)(2,1)} fusion(bf16[129,1792]{1,0:T(8,128)(2,1)S(1)} %concatenate.12, s32[2048]{0:T(1024)S(1)} %pad_clamp_fusion), kind=kCustom, calls=%fused_computation | custom fusion | bytes 11016192 | tf_op jit(solution)/shard_map/gather | solution.py:80
  14.5 7.1 %all-to-all-start = ((bf16[16,96,1792]{2,1,0:T(8,128)(2,1)}), bf16[16,96,1792]{2,1,0:T(8,128)(2,1)}, u32[]{:S(2)}, u32[]{:S(2)}) async-start(bf16[16,96,1792]{2,1,0:T(8,128)(2,1)} %bitcast.23), calls=%async_computation | async-start | bytes 11010048 | tf_op jit(solution)/shard_map/all_to_all | solution.py:81
  21.6 4.8 %slice.12 = bf16[1,1,1024,2048]{3,2,1,0:T(8,128)(2,1)} slice(bf16[1,1,1792,2048]{3,2,1,0:T(8,128)(2,1)} %param.9), slice={[0:1], [0:1], [0:1024], [0:2048]} | slice | bytes 8388608 | tf_op jit(solution)/shard_map/slice | solution.py:99
  26.4 0.6 collective-permute-start
  27.0 0.6 collective-permute-start.1
  27.5 147.8 %collective-permute-done = bf16[1,1,1024,2048]{3,2,1,0:T(8,128)(2,1)} collective-permute-done((bf16[1,1,1024,2048]{3,2,1,0:T(8,128)(2,1)}, bf16[1,1,1024,2048]{3,2,1,0:T(8,128)(2,1)}, u32[]{:S(2)}, u32[]{:S(2)}) %collective-permute-start) | collective-permute-done | bytes 4194336 | tf_op jit(solution)/shard_map/ppermute | solution.py:14
  175.3 16.1 %fusion.1 = f32[1536,2048]{1,0:T(8,128)S(1)} fusion(bf16[1536,1792]{1,0:T(8,128)(2,1)} %bitcast.2, bf16[1,1,1792,2048]{3,2,1,0:T(8,128)(2,1)} %param.9), kind=kOutput, calls=%fused_computation.7 | convolution fusion | flops 11274289152 | bytes 25427968 | tf_op jit(solution)/shard_map/dot_general | solution.py:42
  191.4 3.4 constant_dynamic-slice_fusion
  194.9 3.0 copy-done.3
  198.2 10.2 %collective-permute-done.2 = f32[768,2048]{1,0:T(8,128)} collective-permute-done((f32[768,2048]{1,0:T(8,128)}, f32[768,2048]{1,0:T(8,128)}, u32[]{:S(2)}, u32[]{:S(2)}) %collective-permute-start.2) | collective-permute-done | bytes 6291488 | tf_op jit(solution)/shard_map/ppermute | solution.py:14
  208.4 5.9 %dynamic-slice_add_fusion = f32[768,2048]{1,0:T(8,128)S(1)} fusion(f32[768,2048]{1,0:T(8,128)} %collective-permute-done.2, f32[1536,2048]{1,0:T(8,128)} %copy-done.3, s32[]{:T(128)S(6)} %select_n.73), kind=kLoop, calls=%fused_computation.9 | loop fusion | flops 1572864 | bytes 18874372 | tf_op jit(solution)/shard_map/add | solution.py:46
  214.3 2.7 fusion.6
  216.9 0.5 copy-done.2
  217.6 3.5 collective-permute-done.3
  221.1 4.3 broadcast_select_fusion.1
  225.7 54.2 %collective-permute-done.4 = bf16[1,1024,1792]{2,1,0:T(8,128)(2,1)} collective-permute-done((bf16[1,1024,1792]{2,1,0:T(8,128)(2,1)}, bf16[1,1024,1792]{2,1,0:T(8,128)(2,1)}, u32[]{:S(2)}, u32[]{:S(2)}) %collective-permute-start.4) | collective-permute-done | bytes 3670048 | tf_op jit(solution)/shard_map/ppermute | solution.py:14
  279.9 9.6 %convolution_convert_fusion = bf16[768,2,1792]{2,0,1:T(8,128)(2,1)} fusion(bf16[1,1024,1792]{2,1,0:T(8,128)(2,1)} %param.10, bf16[96,2,8,1024]{3,2,1,0:T(8,128)(2,1)S(1)} %bitcast.25), kind=kOutput, calls=%fused_computation.10 | convolution fusion | flops 5639897088 | bytes 12320768 | tf_op jit(solution)/shard_map/rqhk,qkc->hrc/dot_general | solution.py:53
  289.6 8.0 %all-to-all-start.1 = ((bf16[16,96,1792]{2,1,0:T(8,128)(2,1)}), bf16[16,96,1792]{2,1,0:T(8,128)(2,1)}, u32[]{:S(2)}, u32[]{:S(2)}) async-start(bf16[16,96,1792]{2,1,0:T(8,128)(2,1)} %bitcast.24), calls=%async_computation.1 | async-start | bytes 11010048 | tf_op jit(solution)/shard_map/all_to_all | solution.py:88
  297.5 4.0 slice.15
  301.5 0.6 collective-permute-start.6
  302.1 0.6 collective-permute-start.7
  302.6 0.6 dynamic_slice.18
  304.6 119.9 %collective-permute-done.6 = bf16[1,1,768,2048]{3,2,1,0:T(8,128)(2,1)} collective-permute-done((bf16[1,1,768,2048]{3,2,1,0:T(8,128)(2,1)}, bf16[1,1,768,2048]{3,2,1,0:T(8,128)(2,1)}, u32[]{:S(2)}, u32[]{:S(2)}) %collective-permute-start.6) | collective-permute-done | bytes 3145760 | tf_op jit(solution)/shard_map/ppermute | solution.py:14
  424.5 2.9 collective-permute-done.7
  427.4 11.0 %maximum_select_fusion = bf16[1,1,1792,2048]{3,2,1,0:T(8,128)(2,1)} fusion(bf16[1,1,768,2048]{3,2,1,0:T(8,128)(2,1)} %collective-permute-done.6, bf16[1,1,1024,2048]{3,2,1,0:T(8,128)(2,1)} %collective-permute-done.1, bf16[1,1,1792,2048]{3,2,1,0:T(8,128)(2,1)} %param.9, bf16[1,1,768,2048]{3,2,1,0:T(8,128)(2,1)} %collective-permute-done.7, ...), kind=kLoop, calls=%fused_computation.3 | loop fusion | flops 36700160 | bytes 29360130 | tf_op jit(solution)/shard_map/jit(_where)/select_n | solution.py:22
  438.5 5.5 %select_select_fusion = bf16[1,1024,1792]{2,1,0:T(8,128)(2,1)} fusion(bf16[1,1024,1792]{2,1,0:T(8,128)(2,1)} %collective-permute-done.5, bf16[1,1024,1792]{2,1,0:T(8,128)(2,1)} %collective-permute-done.4, bf16[1,1024,1792]{2,1,0:T(8,128)(2,1)} %param.10, pred[]{:T(512)S(6)} %eq.30, pred[]{:T(512)S(6)} %eq.29), kind=kLoop, calls=%fused_computation.12 | loop fusion | flops 3670016 | bytes 14680066 | tf_op jit(solution)/shard_map/jit(_where)/select_n | solution.py:22
  443.9 11.4 %gather_fusion.1 = bf16[1024,1792]{1,0:T(8,128)(2,1)} fusion(bf16[1536,1792]{1,0:T(8,128)(2,1)} %bitcast.8, s32[1024]{0:T(1024)S(1)} %broadcast_clamp_fusion), kind=kCustom, calls=%fused_computation.1 | custom fusion | bytes 7344128 | tf_op jit(solution)/shard_map/gather | solution.py:89
  455.3 6.1 %fusion = bf16[128,1792]{1,0:T(8,128)(2,1)} fusion(bf16[1024,1792]{1,0:T(8,128)(2,1)} %gather_fusion.1, f32[128,8]{1,0:T(8,128)S(1)} %copy.20), kind=kLoop, calls=%fused_computation.6 | loop fusion | flops 5275648 | bytes 4132864 | tf_op jit(solution)/shard_map/reduce_sum | solution.py:92
  (32 shorter events, 1.5 us)
Async XLA Ops:
  0.6 7.1 %copy-start = (bf16[128,3584]{1,0:T(8,128)(2,1)S(1)}, bf16[128,3584]{1,0:T(8,128)(2,1)}, u32[]{:S(2)}) copy-start(bf16[128,3584]{1,0:T(8,128)(2,1)} %param.6) | copy-start | bytes 2752516
  14.5 160.8 %all-to-all-start = ((bf16[16,96,1792]{2,1,0:T(8,128)(2,1)}), bf16[16,96,1792]{2,1,0:T(8,128)(2,1)}, u32[]{:S(2)}, u32[]{:S(2)}) async-start(bf16[16,96,1792]{2,1,0:T(8,128)(2,1)} %bitcast.23), calls=%async_computation | async-start | bytes 11010048 | tf_op jit(solution)/shard_map/all_to_all | solution.py:81
  26.4 148.9 %collective-permute-start = (bf16[1,1,1024,2048]{3,2,1,0:T(8,128)(2,1)}, bf16[1,1,1024,2048]{3,2,1,0:T(8,128)(2,1)}, u32[]{:S(2)}, u32[]{:S(2)}) collective-permute-start(bf16[1,1,1024,2048]{3,2,1,0:T(8,128)(2,1)} %slice.12), channel_id=1, source_target_pairs={{0,2},{2,0},{4,6},{6,4},{8,10},{10,8},{12,14},{14,12},{16,18},{18,... | collective-permute-start | bytes 12582920 | tf_op jit(solution)/shard_map/ppermute | solution.py:14
  27.0 148.3 %collective-permute-start.1 = (bf16[1,1,1024,2048]{3,2,1,0:T(8,128)(2,1)}, bf16[1,1,1024,2048]{3,2,1,0:T(8,128)(2,1)}, u32[]{:S(2)}, u32[]{:S(2)}) collective-permute-start(bf16[1,1,1024,2048]{3,2,1,0:T(8,128)(2,1)} %slice.12), channel_id=1, source_target_pairs={{0,4},{4,0},{2,6},{6,2},{8,12},{12,8},{10,14},{14,10},{16,20},{20,... | collective-permute-start | bytes 12582920 | tf_op jit(solution)/shard_map/ppermute | solution.py:14
  191.4 6.4 %copy-start.3 = (f32[1536,2048]{1,0:T(8,128)}, f32[1536,2048]{1,0:T(8,128)S(1)}, u32[]{:S(2)}) copy-start(f32[1536,2048]{1,0:T(8,128)S(1)} %fusion.1) | copy-start | bytes 37748740
  197.9 10.5 %collective-permute-start.2 = (f32[768,2048]{1,0:T(8,128)}, f32[768,2048]{1,0:T(8,128)}, u32[]{:S(2)}, u32[]{:S(2)}) collective-permute-start(f32[768,2048]{1,0:T(8,128)} %constant_dynamic-slice_fusion), channel_id=1, source_target_pairs={{0,1},{1,0},{2,3},{3,2},{4,5},{5,4},{6,7},{7,6},{8,9},{9,8},{10,11... | collective-permute-start | bytes 18874376 | tf_op jit(solution)/shard_map/ppermute | solution.py:14
  197.9 82.1 %collective-permute-start.4 = (bf16[1,1024,1792]{2,1,0:T(8,128)(2,1)}, bf16[1,1024,1792]{2,1,0:T(8,128)(2,1)}, u32[]{:S(2)}, u32[]{:S(2)}) collective-permute-start(bf16[1,1024,1792]{2,1,0:T(8,128)(2,1)} %param.10), channel_id=1, source_target_pairs={{0,2},{2,0},{4,6},{6,4},{8,10},{10,8},{12,14},{14,12},{16,18},{18,... | collective-permute-start | bytes 11010056 | tf_op jit(solution)/shard_map/ppermute | solution.py:14
  197.9 82.1 %collective-permute-start.5 = (bf16[1,1024,1792]{2,1,0:T(8,128)(2,1)}, bf16[1,1024,1792]{2,1,0:T(8,128)(2,1)}, u32[]{:S(2)}, u32[]{:S(2)}) collective-permute-start(bf16[1,1024,1792]{2,1,0:T(8,128)(2,1)} %param.10), channel_id=1, source_target_pairs={{0,4},{4,0},{2,6},{6,2},{8,12},{12,8},{10,14},{14,10},{16,20},{20,... | collective-permute-start | bytes 11010056 | tf_op jit(solution)/shard_map/ppermute | solution.py:14
  214.3 3.2 copy-start.2
  217.5 3.6 collective-permute-start.3
  289.6 154.4 %all-to-all-start.1 = ((bf16[16,96,1792]{2,1,0:T(8,128)(2,1)}), bf16[16,96,1792]{2,1,0:T(8,128)(2,1)}, u32[]{:S(2)}, u32[]{:S(2)}) async-start(bf16[16,96,1792]{2,1,0:T(8,128)(2,1)} %bitcast.24), calls=%async_computation.1 | async-start | bytes 11010048 | tf_op jit(solution)/shard_map/all_to_all | solution.py:88
  297.5 5.1 %copy-start.5 = (s32[16]{0:T(128)S(1)}, s32[16]{0:T(128)}, u32[]{:S(2)}) copy-start(s32[16]{0:T(128)} %param.11) | copy-start | bytes 196
  297.5 7.0 %copy-start.4 = (f32[128,8]{0,1:T(8,128)S(1)}, f32[128,8]{0,1:T(8,128)}, u32[]{:S(2)}) copy-start(f32[128,8]{0,1:T(8,128)} %param.8) | copy-start | bytes 12292
  301.5 123.0 %collective-permute-start.6 = (bf16[1,1,768,2048]{3,2,1,0:T(8,128)(2,1)}, bf16[1,1,768,2048]{3,2,1,0:T(8,128)(2,1)}, u32[]{:S(2)}, u32[]{:S(2)}) collective-permute-start(bf16[1,1,768,2048]{3,2,1,0:T(8,128)(2,1)} %slice.15), channel_id=1, source_target_pairs={{0,4},{4,0},{2,6},{6,2},{8,12},{12,8},{10,14},{14,10},{16,20},{20,... | collective-permute-start | bytes 9437192 | tf_op jit(solution)/shard_map/ppermute | solution.py:14
  302.1 125.4 %collective-permute-start.7 = (bf16[1,1,768,2048]{3,2,1,0:T(8,128)(2,1)}, bf16[1,1,768,2048]{3,2,1,0:T(8,128)(2,1)}, u32[]{:S(2)}, u32[]{:S(2)}) collective-permute-start(bf16[1,1,768,2048]{3,2,1,0:T(8,128)(2,1)} %slice.15), channel_id=1, source_target_pairs={{0,2},{2,0},{4,6},{6,4},{8,10},{10,8},{12,14},{14,12},{16,18},{18,... | collective-permute-start | bytes 9437192 | tf_op jit(solution)/shard_map/ppermute | solution.py:14
  443.9 17.5 %copy-start.1 = (bf16[128,3584]{1,0:T(8,128)(2,1)S(1)}, bf16[128,3584]{1,0:T(8,128)(2,1)}, u32[]{:S(2)}) copy-start(bf16[128,3584]{1,0:T(8,128)(2,1)} %param.6) | copy-start | bytes 2752516

commit v2 on v1

--- a/solution.py
+++ b/solution.py
@@ -27,6 +27,10 @@
     return [from_partner(block, "expert", bit_number) for bit_number in range(2)]
 
 
+def tie(value, *moved):
+    return lax.optimization_barrier((value, *moved))
+
+
 def joined(block):
     if lax.axis_size("dp") > 2:
         return lax.all_gather(block, "dp", axis=1, tiled=True)
@@ -37,9 +41,27 @@
     second = jnp.where(side == 0, other, block)
     return jnp.concatenate([first, second], axis=1)
 
+def move_parts(block, shares, axis):
+    unit = block.shape[axis] // sum(shares)
+    parts, start = [], 0
+    for share in shares:
+        parts.append(move(lax.slice_in_dim(block, start, start + share * unit, axis=axis)))
+        start += share * unit
+    return parts
 
-def expert_mlp(flat, gate_up, down, side, moved):
+
+def gather_parts(block, parts, partner, axis):
+    result, start = block, 0
+    for part in parts:
+        width = part[0].shape[axis]
+        own = lax.slice_in_dim(block, start, start + width, axis=axis)
+        result = lax.dynamic_update_slice_in_dim(result, pick(own, part, partner), start, axis)
+        start += width
+    return result
+
+def expert_mlp(flat, gate_up, down, side, gate_up_parts, down_parts):
     partial_value = jnp.dot(flat, gate_up, preferred_element_type=jnp.float32)
+    partial_value, down_parts[0] = tie(partial_value, down_parts[0])
     half_rows = flat.shape[0] // 2
     mine = lax.dynamic_slice_in_dim(partial_value, side * half_rows, half_rows, 0)
     other = lax.dynamic_slice_in_dim(partial_value, (1 - side) * half_rows, half_rows, 0)
@@ -47,7 +69,7 @@
     block_units = gate_up.shape[1] // 2
     hidden = (jax.nn.silu(summed[:, :block_units]) * summed[:, block_units:]).astype(jnp.bfloat16)
     gathered = joined(hidden)
-    gathered, moved = lax.optimization_barrier((gathered, moved))
+    gathered, down_parts[1] = tie(gathered, down_parts[1])
     pair_count = lax.axis_size("dp") // 2
     out_columns = down.shape[1]
     outputs = jnp.einsum(
@@ -56,10 +78,10 @@
         down.reshape(pair_count, block_units, out_columns),
         preferred_element_type=jnp.float32,
     )
-    return outputs.reshape(2 * half_rows, out_columns), moved
+    return outputs.reshape(2 * half_rows, out_columns)
 
 
-def run_layer(tokens, expert_ids, route_weights, gate_up, down, moved):
+def run_layer(tokens, expert_ids, route_weights, gate_up, down, gate_up_parts, down_parts):
     devices = lax.axis_size("expert")
     token_rows, model_width = tokens.shape
     top_count = expert_ids.shape[1]
@@ -78,30 +100,32 @@
     source = jnp.full((devices * capacity,), token_rows, jnp.int32).at[place].set(row_ids)
     padded = jnp.concatenate([own_half, jnp.zeros((1, half_width), own_half.dtype)], axis=0)
     outgoing = padded[source].reshape(devices, capacity, half_width)
+    outgoing, gate_up_parts[0] = tie(outgoing, gate_up_parts[0])
     arrived = lax.all_to_all(outgoing, "expert", split_axis=0, concat_axis=0, tiled=True)
     flat = arrived.reshape(devices * capacity, half_width)
-    (early, middle) = moved
-    flat, early = lax.optimization_barrier((flat, early))
-    outputs, middle = expert_mlp(flat, gate_up, down, side, middle)
+    flat, gate_up_parts[1] = tie(flat, gate_up_parts[1])
+    outputs = expert_mlp(flat, gate_up, down, side, gate_up_parts, down_parts)
     out_columns = down.shape[1]
     expert_out = outputs.reshape(devices, capacity, out_columns).astype(jnp.bfloat16)
+    expert_out, gate_up_parts[2] = tie(expert_out, gate_up_parts[2])
     returned = lax.all_to_all(expert_out, "expert", split_axis=0, concat_axis=0, tiled=True)
+    returned, gate_up_parts[3] = tie(returned, gate_up_parts[3])
     chosen = returned.reshape(devices * capacity, out_columns)[place].reshape(
         token_rows, top_count, out_columns
     )
     mixed = jnp.sum(chosen.astype(jnp.float32) * route_weights[:, :, None], axis=1)
-    return mixed.astype(jnp.bfloat16), (early, middle)
+    mixed, gate_up_parts[4] = tie(mixed.astype(jnp.bfloat16), gate_up_parts[4])
+    return mixed
 
 
 def per_device(tokens, expert_ids, route_weights, gate_up_panels, down_panels, partner):
-    cut = gate_up_panels.shape[2] // 7 * 4
-    moe_out, moved = run_layer(
-        tokens, expert_ids, route_weights, gate_up_panels[0, 0], down_panels[0], (move(gate_up_panels[:, :, :cut]), move(down_panels))
+    gate_up_parts = move_parts(gate_up_panels, (1, 5, 1, 5, 2), 2)
+    down_parts = move_parts(down_panels, (1, 3), 1)
+    moe_out = run_layer(
+        tokens, expert_ids, route_weights, gate_up_panels[0, 0], down_panels[0], gate_up_parts, down_parts
     )
-    late = move(gate_up_panels[:, :, cut:])
-    whole = [jnp.concatenate(parts, axis=2) for parts in zip(moved[0], late)]
-    new_gate_up = pick(gate_up_panels, whole, partner)
-    new_down = pick(down_panels, moved[1], partner)
+    new_gate_up = gather_parts(gate_up_panels, gate_up_parts, partner, 2)
+    new_down = gather_parts(down_panels, down_parts, partner, 1)
     return (moe_out, new_gate_up, new_down)
 
 

time: 463 us -> 404 us (0.87)
  waiting for transfers between devices: 338 us -> 254 us
  other arithmetic: 38 us -> 49.5 us
  local copies, waits for them, and re-layouts: 39.1 us -> 50 us
  starting transfers between devices: 17.8 us -> 22.9 us
    ppermute x8 -> x16, waiting for transfers between devices: 338 us -> 238 us  [from_partner(): return lax.ppermute(block, axis, route)]
    dynamic_update_slice x0 -> x7, other arithmetic: none -> 28.1 us  [gather_parts(): lax.dynamic_update_slice_in_dim(result, pick(own, part, partner), start,...]
    select_n x2 -> x0, other arithmetic: 16.5 us -> none  [pick(): result = jnp.where(taken, moved[bit_number], result)]
    unnamed x13 -> x31, local copies, waits for them, and re-layouts: 3.65 us -> 14.9 us
    all_to_all x1, waiting for transfers between devices: 0.01 us -> 8.85 us  [run_layer(): lax.all_to_all(expert_out, 'expert', split_axis=0, concat_axis=0, tiled=T...]
    ppermute x8 -> x16, starting transfers between devices: 2.68 us -> 9.49 us  [from_partner(): return lax.ppermute(block, axis, route)]
    all_to_all x1, waiting for transfers between devices: 0.01 us -> 6.53 us  [run_layer(): lax.all_to_all(outgoing, 'expert', split_axis=0, concat_axis=0, tiled=True)]
  transfers between devices with their start and end apart: 10 -> 18, of which waited for: 6 -> 11; matrix products, arithmetic and copies ran while one was open for 8% -> 26% of each run, Pallas kernels for 0% -> 0%
where the time goes in v2:
time: 404 us; the launch traced here: 402 us
  waiting for transfers between devices  254 us (63%)
  local copies, waits for them, and re-layouts  50 us (12%)
  other arithmetic  49.5 us (12%)
  matrix products  23.9 us (6%)
  starting transfers between devices  22.9 us (6%)
    ppermute x16, waiting for transfers between devices, from_partner(): return lax.ppermute(block, axis, route)  238 us
    dynamic_update_slice x7, other arithmetic, gather_parts(): lax.dynamic_update_slice_in_dim(result, pick(own, part, partner), start,...  28.1 us
    dot_general x1, matrix products, expert_mlp(): partial_value = jnp.dot(flat, gate_up, preferred_element_type=jnp.float32)  16.1 us
    unnamed x31, local copies, waits for them, and re-layouts  14.9 us
    gather x1, local copies, waits for them, and re-layouts, run_layer(): returned.reshape(devices * capacity, out_columns)[place]  11.2 us
    ppermute x16, starting transfers between devices, from_partner(): return lax.ppermute(block, axis, route)  9.49 us
    all_to_all x1, waiting for transfers between devices, run_layer(): lax.all_to_all(expert_out, 'expert', split_axis=0, concat_axis=0, tiled=T...  8.85 us
    slice x5, local copies, waits for them, and re-layouts, move_parts(): lax.slice_in_dim(block, start, start + share * unit, axis=axis)  8.45 us
  transfers between devices with their start and end apart: 18, of which 11 were waited for; matrix products, arithmetic and copies ran while one was open for 26% of the time, Pallas kernels for 0%

profile of v2, /device:TPU:14, one launch (start us, length us, event | category | flops | bytes accessed | tf_op | source)
XLA Modules:
  0.0 402.2 jit_solution(15747934549962322146)
XLA Ops:
  5.7 4.3 %scatter_custom_fusion = s32[1536]{0:T(1024)S(1)} fusion(s32[1024]{0:T(1024)S(1)} %bitcast.26, s32[1024]{0:T(1024)S(1)} %reshape.92, s32[]{:T(128)} %constant.8.clone.1), kind=kCustom, calls=%fused_computation.35 | custom fusion | bytes 6148 | tf_op jit(solution)/shard_map/scatter | solution.py:100
  10.0 6.6 %gather_fusion = bf16[1536,1792]{1,0:T(8,128)(2,1)} fusion(bf16[129,1792]{1,0:T(8,128)(2,1)S(1)} %concatenate.6, s32[2048]{0:T(1024)S(1)} %pad_clamp_fusion), kind=kCustom, calls=%fused_computation | custom fusion | bytes 11016192 | tf_op jit(solution)/shard_map/gather | solution.py:102
  17.6 7.2 %all-to-all-start = ((bf16[16,96,1792]{2,1,0:T(8,128)(2,1)}), bf16[16,96,1792]{2,1,0:T(8,128)(2,1)}, u32[]{:S(2)}, u32[]{:S(2)}) async-start(bf16[16,96,1792]{2,1,0:T(8,128)(2,1)} %bitcast.23), calls=%async_computation | async-start | bytes 11010048 | tf_op jit(solution)/shard_map/all_to_all | solution.py:104
  24.9 1.9 slice.35
  32.2 98.1 %collective-permute-done.2 = bf16[1,1,640,2048]{3,2,1,0:T(8,128)(2,1)} collective-permute-done((bf16[1,1,640,2048]{3,2,1,0:T(8,128)(2,1)S(1)}, bf16[1,1,640,2048]{3,2,1,0:T(8,128)(2,1)}, u32[]{:S(2)}, u32[]{:S(2)}) %collective-permute-start.2) | collective-permute-done | bytes 2621472 | tf_op jit(solution)/shard_map/ppermute | solution.py:14
  130.3 11.1 %collective-permute-done.3 = bf16[1,1,640,2048]{3,2,1,0:T(8,128)(2,1)} collective-permute-done((bf16[1,1,640,2048]{3,2,1,0:T(8,128)(2,1)S(1)}, bf16[1,1,640,2048]{3,2,1,0:T(8,128)(2,1)}, u32[]{:S(2)}, u32[]{:S(2)}) %collective-permute-start.3) | collective-permute-done | bytes 2621472 | tf_op jit(solution)/shard_map/ppermute | solution.py:14
  141.4 6.5 %all-to-all-done = bf16[16,96,1792]{2,1,0:T(8,128)(2,1)} async-done(((bf16[16,96,1792]{2,1,0:T(8,128)(2,1)}), bf16[16,96,1792]{2,1,0:T(8,128)(2,1)}, u32[]{:S(2)}, u32[]{:S(2)}) %all-to-all-start) | async-done | bytes 5505056 | tf_op jit(solution)/shard_map/all_to_all | solution.py:104
  147.9 16.1 %fusion.1 = f32[1536,2048]{1,0:T(8,128)S(1)} fusion(bf16[1536,1792]{1,0:T(8,128)(2,1)} %bitcast.2, bf16[1,1,1792,2048]{3,2,1,0:T(8,128)(2,1)} %param.9), kind=kOutput, calls=%fused_computation.5 | convolution fusion | flops 11274289152 | bytes 25427968 | tf_op jit(solution)/shard_map/dot_general | solution.py:63
  164.1 3.4 constant_dynamic-slice_fusion
  167.5 3.9 copy-done.7
  173.2 8.8 %collective-permute-done.6 = f32[768,2048]{1,0:T(8,128)} collective-permute-done((f32[768,2048]{1,0:T(8,128)}, f32[768,2048]{1,0:T(8,128)}, u32[]{:S(2)}, u32[]{:S(2)}) %collective-permute-start.6) | collective-permute-done | bytes 6291488 | tf_op jit(solution)/shard_map/ppermute | solution.py:14
  181.9 5.9 %dynamic-slice_add_fusion = f32[768,2048]{1,0:T(8,128)S(1)} fusion(f32[768,2048]{1,0:T(8,128)} %collective-permute-done.6, f32[1536,2048]{1,0:T(8,128)} %copy-done.7, s32[]{:T(128)S(6)} %select_n.141), kind=kLoop, calls=%fused_computation.7 | loop fusion | flops 1572864 | bytes 18874372 | tf_op jit(solution)/shard_map/add | solution.py:68
  187.9 2.6 fusion.6
  191.1 7.6 %copy.26 = bf16[1,1,1792,2048]{3,2,1,0:T(8,128)(2,1)} copy(bf16[1,1,1792,2048]{3,2,1,0:T(8,128)(2,1)} %param.9) | data formatting | bytes 14680064
  200.6 2.3 select_dynamic-update-slice_fusion.6
  202.9 4.3 %broadcast_select_fusion.1 = (bf16[768,1024]{1,0:T(8,128)(2,1)S(1)}, bf16[768,1024]{1,0:T(8,128)(2,1)S(1)}) fusion(bf16[768,1024]{1,0:T(8,128)(2,1)S(1)} %collective-permute-done.7, pred[]{:T(512)S(6)} %eq.12, f32[768,2048]{1,0:T(8,128)} %copy-done.2), kind=kLoop, calls=%fused_computation.19 | loop fusion | flops 6291456 | bytes 11010049 | tf_op jit(solution)/shard_map/jit(_where)/select_n | solution.py:40
  207.6 28.4 %collective-permute-done.8 = bf16[1,768,1792]{2,1,0:T(8,128)(2,1)} collective-permute-done((bf16[1,768,1792]{2,1,0:T(8,128)(2,1)}, bf16[1,768,1792]{2,1,0:T(8,128)(2,1)}, u32[]{:S(2)}, u32[]{:S(2)}) %collective-permute-start.8) | collective-permute-done | bytes 2752544 | tf_op jit(solution)/shard_map/ppermute | solution.py:14
  236.0 7.6 %convolution_convert_fusion = bf16[768,2,1792]{2,0,1:T(8,128)(2,1)} fusion(bf16[1,1024,1792]{2,1,0:T(8,128)(2,1)S(1)} %copy-done.4, bf16[96,2,8,1024]{3,2,1,0:T(8,128)(2,1)S(1)} %bitcast.25), kind=kOutput, calls=%fused_computation.8 | convolution fusion | flops 5639897088 | bytes 12320768 | tf_op jit(solution)/shard_map/rqhk,qkc->hrc/dot_general | solution.py:75
  243.6 3.1 collective-permute-done.10
  246.8 6.2 %all-to-all-start.1 = ((bf16[16,96,1792]{2,1,0:T(8,128)(2,1)}), bf16[16,96,1792]{2,1,0:T(8,128)(2,1)}, u32[]{:S(2)}, u32[]{:S(2)}) async-start(bf16[16,96,1792]{2,1,0:T(8,128)(2,1)} %bitcast.24), calls=%async_computation.1 | async-start | bytes 11010048 | tf_op jit(solution)/shard_map/all_to_all | solution.py:111
  253.0 8.3 %select_dynamic-update-slice_fusion.2 = (bf16[1,1,1792,2048]{3,2,1,0:T(8,128)(2,1)}, bf16[1,1,640,2048]{3,2,1,0:T(8,128)(2,1)}) fusion(bf16[1,1,1792,2048]{3,2,1,0:T(8,128)(2,1)} %get-tuple-element.47, bf16[1,1,640,2048]{3,2,1,0:T(8,128)(2,1)} %collective-permute-done.3, bf16[1,1,640,2048]{3,2,1,0:T(8,128)(2,1)} %collective-permute-done.2, pred[]{:T(512)S(6)} %eq.17, ...), kind=kLoop, calls=%fused_computation.17 | loop fusion | flops 2621440 | bytes 15728642 | tf_op jit(solution)/shard_map/dynamic_update_slice | solution.py:58
  262.5 2.4 slice.42
  269.8 2.9 select_dynamic-update-slice_fusion.4
  272.6 2.1 select_dynamic-update-slice_fusion.5
  274.7 4.5 %select_dynamic-update-slice_fusion = bf16[1,1024,1792]{2,1,0:T(8,128)(2,1)} fusion(bf16[1,1024,1792]{2,1,0:T(8,128)(2,1)} %select_dynamic-update-slice_fusion.4, bf16[1,768,1792]{2,1,0:T(8,128)(2,1)} %collective-permute-done.9, bf16[1,768,1792]{2,1,0:T(8,128)(2,1)} %collective-permute-done.8, pred[]{:T(512)S(6)} %eq.17, pred[]{:T(512)S(6)} %eq.16, ...), kind=kLoop, calls=%fused_computation.15 | loop fusion | flops 2752512 | bytes 11010050 | tf_op jit(solution)/shard_map/dynamic_update_slice | solution.py:58
  279.2 79.5 %collective-permute-done.12 = bf16[1,1,640,2048]{3,2,1,0:T(8,128)(2,1)S(1)} collective-permute-done((bf16[1,1,640,2048]{3,2,1,0:T(8,128)(2,1)}, bf16[1,1,640,2048]{3,2,1,0:T(8,128)(2,1)S(1)}, u32[]{:S(2)}, u32[]{:S(2)}) %collective-permute-start.12) | collective-permute-done | bytes 2621472 | tf_op jit(solution)/shard_map/ppermute | solution.py:14
  358.7 8.7 %collective-permute-done.13 = bf16[1,1,640,2048]{3,2,1,0:T(8,128)(2,1)} collective-permute-done((bf16[1,1,640,2048]{3,2,1,0:T(8,128)(2,1)}, bf16[1,1,640,2048]{3,2,1,0:T(8,128)(2,1)}, u32[]{:S(2)}, u32[]{:S(2)}) %collective-permute-start.13) | collective-permute-done | bytes 2621472 | tf_op jit(solution)/shard_map/ppermute | solution.py:14
  367.4 8.9 %all-to-all-done.1 = bf16[16,96,1792]{2,1,0:T(8,128)(2,1)} async-done(((bf16[16,96,1792]{2,1,0:T(8,128)(2,1)}), bf16[16,96,1792]{2,1,0:T(8,128)(2,1)}, u32[]{:S(2)}, u32[]{:S(2)}) %all-to-all-start.1) | async-done | bytes 5505056 | tf_op jit(solution)/shard_map/all_to_all | solution.py:111
  376.3 11.2 %gather_fusion.1 = bf16[1024,1792]{1,0:T(8,128)(2,1)} fusion(bf16[1536,1792]{1,0:T(8,128)(2,1)} %bitcast.8, s32[1024]{0:T(1024)S(1)} %broadcast_clamp_fusion), kind=kCustom, calls=%fused_computation.1 | custom fusion | bytes 7344128 | tf_op jit(solution)/shard_map/gather | solution.py:113
  387.5 6.1 %fusion = bf16[128,1792]{1,0:T(8,128)(2,1)} fusion(bf16[1024,1792]{1,0:T(8,128)(2,1)} %gather_fusion.1, f32[128,8]{1,0:T(8,128)S(1)} %copy.20), kind=kLoop, calls=%fused_computation.4 | loop fusion | flops 5275648 | bytes 4132864 | tf_op jit(solution)/shard_map/reduce_sum | solution.py:116
  394.1 5.0 %select_dynamic-update-slice_fusion.1 = bf16[1,1,1792,2048]{3,2,1,0:T(8,128)(2,1)} fusion(bf16[1,1,1792,2048]{3,2,1,0:T(8,128)(2,1)} %select_dynamic-update-slice_fusion.5, bf16[1,1,640,2048]{3,2,1,0:T(8,128)(2,1)} %collective-permute-done.13, bf16[1,1,640,2048]{3,2,1,0:T(8,128)(2,1)S(1)} %collective-permute-done.12, pred[]{:T(512)S(6)} %eq.17, pred[]{:T(512)S(6)} %eq.16, ...), kind=kLoop, calls=%fused_computation.16 | loop fusion | flops 2621440 | bytes 10485762 | tf_op jit(solution)/shard_map/dynamic_update_slice | solution.py:58
  399.1 3.1 select_dynamic-update-slice_fusion.3
  (74 shorter events, 21.2 us)
Async XLA Ops:
  0.6 4.9 %copy-start = (bf16[128,3584]{1,0:T(8,128)(2,1)S(1)}, bf16[128,3584]{1,0:T(8,128)(2,1)}, u32[]{:S(2)}) copy-start(bf16[128,3584]{1,0:T(8,128)(2,1)} %param.6) | copy-start | bytes 2752516
  1.8 14.8 %collective-permute-start = (bf16[1,1,128,2048]{3,2,1,0:T(8,128)(2,1)S(1)}, bf16[1,1,128,2048]{3,2,1,0:T(8,128)(2,1)S(1)}, u32[]{:S(2)}, u32[]{:S(2)}) collective-permute-start(bf16[1,1,128,2048]{3,2,1,0:T(8,128)(2,1)S(1)} %slice.34), channel_id=1, source_target_pairs={{0,2},{2,0},{4,6},{6,4},{8,10},{10,8},{12,14},{14,12},{16,18},{18,... | collective-permute-start | bytes 1572872 | tf_op jit(solution)/shard_map/ppermute | solution.py:14
  2.4 14.3 %collective-permute-start.1 = (bf16[1,1,128,2048]{3,2,1,0:T(8,128)(2,1)S(1)}, bf16[1,1,128,2048]{3,2,1,0:T(8,128)(2,1)S(1)}, u32[]{:S(2)}, u32[]{:S(2)}) collective-permute-start(bf16[1,1,128,2048]{3,2,1,0:T(8,128)(2,1)S(1)} %slice.34), channel_id=1, source_target_pairs={{0,4},{4,0},{2,6},{6,2},{8,12},{12,8},{10,14},{14,10},{16,20},{20,... | collective-permute-start | bytes 1572872 | tf_op jit(solution)/shard_map/ppermute | solution.py:14
  16.7 0.8 copy-start.8
  16.7 1.0 copy-start.10
  17.6 130.3 %all-to-all-start = ((bf16[16,96,1792]{2,1,0:T(8,128)(2,1)}), bf16[16,96,1792]{2,1,0:T(8,128)(2,1)}, u32[]{:S(2)}, u32[]{:S(2)}) async-start(bf16[16,96,1792]{2,1,0:T(8,128)(2,1)} %bitcast.23), calls=%async_computation | async-start | bytes 11010048 | tf_op jit(solution)/shard_map/all_to_all | solution.py:104
  26.8 103.5 %collective-permute-start.2 = (bf16[1,1,640,2048]{3,2,1,0:T(8,128)(2,1)S(1)}, bf16[1,1,640,2048]{3,2,1,0:T(8,128)(2,1)}, u32[]{:S(2)}, u32[]{:S(2)}) collective-permute-start(bf16[1,1,640,2048]{3,2,1,0:T(8,128)(2,1)S(1)} %slice.35), channel_id=1, source_target_pairs={{0,2},{2,0},{4,6},{6,4},{8,10},{10,8},{12,14},{14,12},{16,18},{18,... | collective-permute-start | bytes 7864328 | tf_op jit(solution)/shard_map/ppermute | solution.py:14
  27.4 114.0 %collective-permute-start.3 = (bf16[1,1,640,2048]{3,2,1,0:T(8,128)(2,1)S(1)}, bf16[1,1,640,2048]{3,2,1,0:T(8,128)(2,1)}, u32[]{:S(2)}, u32[]{:S(2)}) collective-permute-start(bf16[1,1,640,2048]{3,2,1,0:T(8,128)(2,1)S(1)} %slice.35), channel_id=1, source_target_pairs={{0,4},{4,0},{2,6},{6,2},{8,12},{12,8},{10,14},{14,10},{16,20},{20,... | collective-permute-start | bytes 7864328 | tf_op jit(solution)/shard_map/ppermute | solution.py:14
  29.2 134.8 %collective-permute-start.4 = (bf16[1,256,1792]{2,1,0:T(8,128)(2,1)S(1)}, bf16[1,256,1792]{2,1,0:T(8,128)(2,1)}, u32[]{:S(2)}, u32[]{:S(2)}) collective-permute-start(bf16[1,256,1792]{2,1,0:T(8,128)(2,1)S(1)} %slice.36), channel_id=1, source_target_pairs={{0,2},{2,0},{4,6},{6,4},{8,10},{10,8},{12,14},{14,12},{16,18},{18,... | collective-permute-start | bytes 2752520 | tf_op jit(solution)/shard_map/ppermute | solution.py:14
  30.8 133.3 %collective-permute-start.5 = (bf16[1,256,1792]{2,1,0:T(8,128)(2,1)S(1)}, bf16[1,256,1792]{2,1,0:T(8,128)(2,1)}, u32[]{:S(2)}, u32[]{:S(2)}) collective-permute-start(bf16[1,256,1792]{2,1,0:T(8,128)(2,1)S(1)} %slice.36), channel_id=1, source_target_pairs={{0,4},{4,0},{2,6},{6,2},{8,12},{12,8},{10,14},{14,10},{16,20},{20,... | collective-permute-start | bytes 2752520 | tf_op jit(solution)/shard_map/ppermute | solution.py:14
  164.1 7.4 %copy-start.7 = (f32[1536,2048]{1,0:T(8,128)}, f32[1536,2048]{1,0:T(8,128)S(1)}, u32[]{:S(2)}) copy-start(f32[1536,2048]{1,0:T(8,128)S(1)} %fusion.1) | copy-start | bytes 37748740
  164.1 7.4 %copy-start.3 = (bf16[1,1024,1792]{2,1,0:T(8,128)(2,1)S(1)}, bf16[1,1024,1792]{2,1,0:T(8,128)(2,1)}, u32[]{:S(2)}) copy-start(bf16[1,1024,1792]{2,1,0:T(8,128)(2,1)} %param.10) | copy-start | bytes 11010052
  171.4 10.5 %collective-permute-start.6 = (f32[768,2048]{1,0:T(8,128)}, f32[768,2048]{1,0:T(8,128)}, u32[]{:S(2)}, u32[]{:S(2)}) collective-permute-start(f32[768,2048]{1,0:T(8,128)} %constant_dynamic-slice_fusion), channel_id=1, source_target_pairs={{0,1},{1,0},{2,3},{3,2},{4,5},{5,4},{6,7},{7,6},{8,9},{9,8},{10,11... | collective-permute-start | bytes 18874376 | tf_op jit(solution)/shard_map/ppermute | solution.py:14
  173.2 62.8 %collective-permute-start.8 = (bf16[1,768,1792]{2,1,0:T(8,128)(2,1)}, bf16[1,768,1792]{2,1,0:T(8,128)(2,1)}, u32[]{:S(2)}, u32[]{:S(2)}) collective-permute-start(bf16[1,768,1792]{2,1,0:T(8,128)(2,1)} %slice.39), channel_id=1, source_target_pairs={{0,2},{2,0},{4,6},{6,4},{8,10},{10,8},{12,14},{14,12},{16,18},{18,... | collective-permute-start | bytes 8257544 | tf_op jit(solution)/shard_map/ppermute | solution.py:14
  173.2 62.8 %collective-permute-start.9 = (bf16[1,768,1792]{2,1,0:T(8,128)(2,1)}, bf16[1,768,1792]{2,1,0:T(8,128)(2,1)}, u32[]{:S(2)}, u32[]{:S(2)}) collective-permute-start(bf16[1,768,1792]{2,1,0:T(8,128)(2,1)} %slice.39), channel_id=1, source_target_pairs={{0,4},{4,0},{2,6},{6,2},{8,12},{12,8},{10,14},{14,10},{16,20},{20,... | collective-permute-start | bytes 8257544 | tf_op jit(solution)/shard_map/ppermute | solution.py:14
  187.9 3.1 copy-start.2
  190.9 12.0 %collective-permute-start.7 = (bf16[768,1024]{1,0:T(8,128)(2,1)}, bf16[768,1024]{1,0:T(8,128)(2,1)S(1)}, u32[]{:S(2)}, u32[]{:S(2)}) collective-permute-start(bf16[768,1024]{1,0:T(8,128)(2,1)} %fusion.6), channel_id=1, source_target_pairs={{0,1},{1,0},{2,3},{3,2},{4,5},{5,4},{6,7},{7,6},{8,9},{9,8},{10,11... | collective-permute-start | bytes 4718600 | tf_op jit(solution)/shard_map/ppermute | solution.py:14
  191.1 7.6 %copy-start.13 = (s32[16]{0:T(128)S(1)}, s32[16]{0:T(128)}, u32[]{:S(2)}) copy-start(s32[16]{0:T(128)} %param.11) | copy-start | bytes 196
  191.1 9.5 %copy-start.9 = (bf16[1,1,128,2048]{3,2,1,0:T(8,128)(2,1)S(1)}, bf16[1,1,128,2048]{3,2,1,0:T(8,128)(2,1)}, u32[]{:S(2)}) copy-start(bf16[1,1,128,2048]{3,2,1,0:T(8,128)(2,1)} %copy-done.8) | copy-start | bytes 1572868
  191.1 9.5 %copy-start.11 = (bf16[1,1,128,2048]{3,2,1,0:T(8,128)(2,1)S(1)}, bf16[1,1,128,2048]{3,2,1,0:T(8,128)(2,1)}, u32[]{:S(2)}) copy-start(bf16[1,1,128,2048]{3,2,1,0:T(8,128)(2,1)} %copy-done.10) | copy-start | bytes 1572868
  202.9 43.8 %collective-permute-start.10 = (bf16[1,1,128,2048]{3,2,1,0:T(8,128)(2,1)S(1)}, bf16[1,1,128,2048]{3,2,1,0:T(8,128)(2,1)S(1)}, u32[]{:S(2)}, u32[]{:S(2)}) collective-permute-start(bf16[1,1,128,2048]{3,2,1,0:T(8,128)(2,1)S(1)} %get-tuple-element.48), channel_id=1, source_target_pairs={{0,2},{2,0},{4,6},{6,4},{8,10},{10,8},{12,14},{14,12},{16,18},{18,... | collective-permute-start | bytes 1572872 | tf_op jit(solution)/shard_map/ppermute | solution.py:14
  202.9 43.9 %collective-permute-start.11 = (bf16[1,1,128,2048]{3,2,1,0:T(8,128)(2,1)S(1)}, bf16[1,1,128,2048]{3,2,1,0:T(8,128)(2,1)}, u32[]{:S(2)}, u32[]{:S(2)}) collective-permute-start(bf16[1,1,128,2048]{3,2,1,0:T(8,128)(2,1)S(1)} %get-tuple-element.48), channel_id=1, source_target_pairs={{0,4},{4,0},{2,6},{6,2},{8,12},{12,8},{10,14},{14,10},{16,20},{20,... | collective-permute-start | bytes 1572872 | tf_op jit(solution)/shard_map/ppermute | solution.py:14
  207.2 28.7 %copy-start.4 = (bf16[1,1024,1792]{2,1,0:T(8,128)(2,1)S(1)}, bf16[1,1024,1792]{2,1,0:T(8,128)(2,1)}, u32[]{:S(2)}) copy-start(bf16[1,1024,1792]{2,1,0:T(8,128)(2,1)} %param.10) | copy-start | bytes 11010052
  246.8 129.4 %all-to-all-start.1 = ((bf16[16,96,1792]{2,1,0:T(8,128)(2,1)}), bf16[16,96,1792]{2,1,0:T(8,128)(2,1)}, u32[]{:S(2)}, u32[]{:S(2)}) async-start(bf16[16,96,1792]{2,1,0:T(8,128)(2,1)} %bitcast.24), calls=%async_computation.1 | async-start | bytes 11010048 | tf_op jit(solution)/shard_map/all_to_all | solution.py:111
  253.0 14.8 %copy-start.5 = (bf16[1,1024,1792]{2,1,0:T(8,128)(2,1)S(1)}, bf16[1,1024,1792]{2,1,0:T(8,128)(2,1)}, u32[]{:S(2)}) copy-start(bf16[1,1024,1792]{2,1,0:T(8,128)(2,1)} %param.10) | copy-start | bytes 11010052
  261.3 97.3 %collective-permute-start.12 = (bf16[1,1,640,2048]{3,2,1,0:T(8,128)(2,1)}, bf16[1,1,640,2048]{3,2,1,0:T(8,128)(2,1)S(1)}, u32[]{:S(2)}, u32[]{:S(2)}) collective-permute-start(bf16[1,1,640,2048]{3,2,1,0:T(8,128)(2,1)} %get-tuple-element.46), channel_id=1, source_target_pairs={{0,2},{2,0},{4,6},{6,4},{8,10},{10,8},{12,14},{14,12},{16,18},{18,... | collective-permute-start | bytes 7864328 | tf_op jit(solution)/shard_map/ppermute | solution.py:14
  261.9 105.5 %collective-permute-start.13 = (bf16[1,1,640,2048]{3,2,1,0:T(8,128)(2,1)}, bf16[1,1,640,2048]{3,2,1,0:T(8,128)(2,1)}, u32[]{:S(2)}, u32[]{:S(2)}) collective-permute-start(bf16[1,1,640,2048]{3,2,1,0:T(8,128)(2,1)} %get-tuple-element.46), channel_id=1, source_target_pairs={{0,4},{4,0},{2,6},{6,2},{8,12},{12,8},{10,14},{14,10},{16,20},{20,... | collective-permute-start | bytes 7864328 | tf_op jit(solution)/shard_map/ppermute | solution.py:14
  264.9 4.8 %copy-start.12 = (f32[128,8]{0,1:T(8,128)S(1)}, f32[128,8]{0,1:T(8,128)}, u32[]{:S(2)}) copy-start(f32[128,8]{0,1:T(8,128)} %param.8) | copy-start | bytes 12292
  264.9 129.2 %collective-permute-start.14 = (bf16[1,1,256,2048]{3,2,1,0:T(8,128)(2,1)}, bf16[1,1,256,2048]{3,2,1,0:T(8,128)(2,1)}, u32[]{:S(2)}, u32[]{:S(2)}) collective-permute-start(bf16[1,1,256,2048]{3,2,1,0:T(8,128)(2,1)} %slice.42), channel_id=1, source_target_pairs={{0,2},{2,0},{4,6},{6,4},{8,10},{10,8},{12,14},{14,12},{16,18},{18,... | collective-permute-start | bytes 3145736 | tf_op jit(solution)/shard_map/ppermute | solution.py:14
  266.4 127.7 %collective-permute-start.15 = (bf16[1,1,256,2048]{3,2,1,0:T(8,128)(2,1)}, bf16[1,1,256,2048]{3,2,1,0:T(8,128)(2,1)}, u32[]{:S(2)}, u32[]{:S(2)}) collective-permute-start(bf16[1,1,256,2048]{3,2,1,0:T(8,128)(2,1)} %slice.42), channel_id=1, source_target_pairs={{0,4},{4,0},{2,6},{6,2},{8,12},{12,8},{10,14},{14,10},{16,20},{20,... | collective-permute-start | bytes 3145736 | tf_op jit(solution)/shard_map/ppermute | solution.py:14
  269.8 5.0 %copy-start.6 = (bf16[1,1024,1792]{2,1,0:T(8,128)(2,1)S(1)}, bf16[1,1024,1792]{2,1,0:T(8,128)(2,1)}, u32[]{:S(2)}) copy-start(bf16[1,1024,1792]{2,1,0:T(8,128)(2,1)} %param.10) | copy-start | bytes 11010052
  394.1 8.1 %copy-start.1 = (bf16[128,3584]{1,0:T(8,128)(2,1)S(1)}, bf16[128,3584]{1,0:T(8,128)(2,1)}, u32[]{:S(2)}) copy-start(bf16[128,3584]{1,0:T(8,128)(2,1)} %param.6) | copy-start | bytes 2752516
